TPU v7x, 32 devices: a whole 2x2x4 slice. The times are simulated.
32 devices in a mesh: dp: 2 (over core), expert: 16 (over z, y, x).
Axes of the slice: x: 2, y: 2, z: 4, core: 2. Of those that a mesh axis runs over, the one named last changes fastest.
Arguments:
- tokens: bfloat16 [2048, 4096], P(('dp', 'expert')), may hold values from -6 to 6
- token_experts: int32 [2048, 8], P(('dp', 'expert')), may hold values from 0 to 15, all different within a row; in each aligned block of 64 rows (0 to 63, 64 to 127, ...) at most 48 rows name the same one
- hidden_grad: bfloat16 [2048, 8, 768], P(('dp', 'expert')), may hold values from -6 to 6
- held_expert: int32 [16], replicated, may hold values from 0 to 15, each once
- swap_mask: int32 [16], replicated, may hold values from 0 to 1, as said below
- weight: bfloat16 [16, 4096, 768], P('expert', 'dp'), may hold values from -0.09375 to 0.09375
- first_moment: float32 [16, 4096, 768], P('expert', 'dp'), may hold values from -57.6 to 57.6
- second_moment: float32 [16, 4096, 768], P('expert', 'dp'), may hold values from 10.24 to 102.4
Outputs:
- token_grad: bfloat16 [2048, 4096], P(('dp', 'expert'))
- adam_step: bfloat16 [16, 4096, 768], P('expert', 'dp')
Inputs may be any that keep to these rules, and one draw needn't show every extreme that they name: `token_experts`: in each aligned block of 64 rows (the tokens of one device) no expert is named by more than 48 rows, and in some blocks one is named by exactly 48; the ids of a row differ. `held_expert`: a permutation of the expert ids. swap_mask[p] equals swap_mask[p + 8] for p below 8, and exactly 2 such pairs are 1.
All inputs are finite; a program needn't handle non-finite values.
Results may differ from a plain program's by a relative error of at most 0.008.
Values may be sent and summed in bfloat16 or wider, within the bound.
A program may use at most 128 MiB of HBM per device.

v0:
```python
import jax
import jax.numpy as jnp
from jax import lax
from jax.sharding import PartitionSpec as P


def passed_along(block, axis, distance):
    devices = range(lax.axis_size(axis))
    route = [((i - distance) % len(devices), i) for i in devices]
    return lax.ppermute(block, axis, route)


def lookup(table, index, lanes):
    return jnp.sum(jnp.where(index[:, None] == lanes[None, :], table[None, :], 0), axis=1)


def adam_direction(grad, first, second):
    first_new = 0.9 * first + 0.1 * grad
    second_new = 0.95 * second + 0.05 * grad * grad
    return (first_new / (jnp.sqrt(second_new) + 1e-08)).astype(jnp.bfloat16)


def body(
    tokens, token_experts, hidden_grad, held_expert, swap_mask, weight, first_moment, second_moment
):
    count_dev = lax.axis_size("expert")
    half_way = count_dev // 2
    here = lax.axis_index("expert")
    tok_dev, top = token_experts.shape
    width = tokens.shape[1]
    hidden = hidden_grad.shape[2]
    capacity = min(tok_dev, 3 * tok_dev * top // (2 * count_dev))
    lanes = jnp.arange(count_dev, dtype=jnp.int32)
    partner = (lanes + half_way) % count_dev
    moving_all = swap_mask == 1
    new_held = jnp.where(moving_all, lookup(held_expert, partner, lanes), held_expert)
    moving = jnp.sum(jnp.where(lanes == here, swap_mask, 0)) == 1
    got_weight = passed_along(weight, "expert", half_way)
    got_first, got_second = (
        passed_along(first_moment.astype(jnp.bfloat16), "expert", half_way).astype(
            first_moment.dtype
        ),
        passed_along(second_moment.astype(jnp.bfloat16), "expert", half_way).astype(
            second_moment.dtype
        ),
    )
    w_shard = jnp.where(moving, got_weight, weight)
    first = jnp.where(moving, got_first, first_moment)
    second = jnp.where(moving, got_second, second_moment)
    owner = jnp.sum(jnp.where(new_held[None, :] == lanes[:, None], lanes[None, :], 0), axis=1)
    full_w = lax.all_gather(w_shard, "dp", axis=1, tiled=True)[0]
    flat_ids = token_experts.reshape(-1)
    dest = lookup(owner, flat_ids, lanes)
    onehot = (dest[:, None] == lanes[None, :]).astype(jnp.int32)
    before = jnp.cumsum(onehot, axis=0) - onehot
    rank = jnp.sum(before * onehot, axis=1)
    slot = dest * capacity + rank
    routed = tok_dev * top
    table = (
        jnp.zeros((count_dev * capacity,), jnp.int32)
        .at[slot]
        .set(jnp.arange(routed, dtype=jnp.int32) + 1)
    )
    filled = table > 0
    source_row = jnp.maximum(table - 1, 0)
    send_x = jnp.where(filled[:, None], tokens[source_row // top], jnp.zeros((), tokens.dtype))
    send_g = jnp.where(
        filled[:, None],
        hidden_grad.reshape(routed, hidden)[source_row],
        jnp.zeros((), hidden_grad.dtype),
    )
    recv_x, recv_g = (
        lax.all_to_all(
            send_x.reshape(count_dev, capacity, width),
            "expert",
            split_axis=0,
            concat_axis=0,
            tiled=True,
        ),
        lax.all_to_all(
            send_g.reshape(count_dev, capacity, hidden),
            "expert",
            split_axis=0,
            concat_axis=0,
            tiled=True,
        ),
    )
    rows_x = recv_x.reshape(count_dev * capacity, width)
    rows_g = recv_g.reshape(count_dev * capacity, hidden)
    pre = jnp.dot(rows_x, full_w, preferred_element_type=jnp.float32)
    sig = jax.nn.sigmoid(pre)
    grad_pre = (rows_g.astype(jnp.float32) * sig * (1.0 + pre * (1.0 - sig))).astype(jnp.bfloat16)
    back_rows = lax.dot_general(
        grad_pre, full_w, (((1,), (1,)), ((), ())), preferred_element_type=jnp.float32
    ).astype(jnp.bfloat16)
    returned = lax.all_to_all(
        back_rows.reshape(count_dev, capacity, width),
        "expert",
        split_axis=0,
        concat_axis=0,
        tiled=True,
    )
    picked = returned.reshape(count_dev * capacity, width)[slot].reshape(tok_dev, top, width)
    token_grad = jnp.sum(picked.astype(jnp.float32), axis=1).astype(jnp.bfloat16)
    expert_grad = lax.psum_scatter(
        lax.dot_general(
            rows_x, grad_pre, (((0,), (0,)), ((), ())), preferred_element_type=jnp.float32
        ).astype(jnp.bfloat16),
        "dp",
        scatter_dimension=0,
        tiled=True,
    ).astype(jnp.float32)
    adam_step = adam_direction(expert_grad, first[0], second[0])[None]
    return (token_grad, adam_step)


def solution(mesh):
    in_specs = (
        P(("dp", "expert"), None),
        P(("dp", "expert"), None),
        P(("dp", "expert"), None, None),
        P(),
        P(),
        P("expert", "dp", None),
        P("expert", "dp", None),
        P("expert", "dp", None),
    )
    out_specs = (P(("dp", "expert"), None), P("expert", "dp", None))
    return jax.shard_map(body, mesh=mesh, in_specs=in_specs, out_specs=out_specs, check_vma=False)
```

profile of v0, /device:TPU:4, one launch (start us, length us, event | category | flops | bytes accessed | tf_op | source)
XLA Modules:
  0.0 808.6 jit_solution(7064839201747426895)
XLA Ops:
  7.2 0.0 copy-start
  7.2 0.9 select_reduce_fusion.2
  8.1 1.3 compare_select_fusion.5
  9.4 0.1 select_reduce_fusion.1
  9.5 0.8 copy.12
  10.3 0.1 eq.80
  10.4 0.1 select_reduce_fusion
  10.5 1.1 reduce-window.6
  11.7 0.2 slice_reduce_fusion
  11.9 0.1 fusion.18
  12.0 2.4 scatter_custom_fusion
  14.5 0.1 broadcast_in_dim.83
  14.6 13.0 %gather_fusion.1 = bf16[768,4096]{1,0:T(8,128)(2,1)} fusion(bf16[64,4096]{1,0:T(8,128)(2,1)} %param.8, s32[1024]{0:T(1024)S(1)} %get-tuple-element.6), kind=kCustom, calls=%fused_computation.1 | custom fusion | bytes 12585984 | tf_op jit(solution)/shard_map/gather | solution.py:66
  27.7 5.9 broadcast_select_fusion
  33.6 7.3 all-to-all-start.1
  40.9 0.0 all-gather.2.cloned.1.call-start
  40.9 2.4 collective-permute-start
  44.0 273.8 %collective-permute-done = bf16[1,2048,768]{2,1,0:T(8,128)(2,1)} collective-permute-done((bf16[1,2048,768]{2,1,0:T(8,128)(2,1)}, bf16[1,2048,768]{2,1,0:T(8,128)(2,1)}, u32[]{:S(2)}, u32[]{:S(2)}) %collective-permute-start) | collective-permute-done | bytes 3145760 | tf_op jit(solution)/shard_map/ppermute | solution.py:10
  317.8 3.9 broadcast_select_fusion.1
  321.6 0.0 all-gather.2.cloned.1.call-update
  321.7 0.0 copy-done
  321.7 2.8 gather_fusion
  324.4 1.2 broadcast_select_fusion.2
  325.7 0.0 all-to-all-done.1
  325.7 4.8 all-to-all-start
  330.4 0.2 reduce-scatter.2.cloned.1.call-start
  330.7 6.9 all-gather.2.cloned.1.call-done
  337.5 10.0 %fusion.7 = f32[768,768]{1,0:T(8,128)} fusion(bf16[768,4096]{1,0:T(8,128)(2,1)} %bitcast.8, bf16[1,4096,768]{2,1,0:T(8,128)(2,1)} %all-gather.2.cloned.1.call-done), kind=kOutput, calls=%fused_computation.15 | convolution fusion | flops 4831838208 | bytes 14942208 | tf_op jit(solution)/shard_map/dot_general | solution.py:90
  347.5 9.0 %all-to-all-done = bf16[16,48,768]{2,1,0:T(8,128)(2,1)S(1)} async-done(((bf16[16,48,768]{2,1,0:T(8,128)(2,1)}), bf16[16,48,768]{2,1,0:T(8,128)(2,1)S(1)}, u32[]{:S(2)}, u32[]{:S(2)}) %all-to-all-start) | async-done | bytes 1179680 | tf_op jit(solution)/shard_map/all_to_all | solution.py:80
  356.5 10.0 %convolution_convert_fusion = bf16[4096,768]{1,0:T(8,128)(2,1)} fusion(bf16[768,4096]{1,0:T(8,128)(2,1)} %bitcast.8, bf16[768,768]{1,0:T(8,128)(2,1)S(1)} %bitcast.53, f32[768,768]{1,0:T(8,128)} %fusion.7), kind=kOutput, calls=%fused_computation.6 | convolution fusion | flops 4840882176 | bytes 16121856 | tf_op jit(solution)/shard_map/dot_general | solution.py:106
  366.5 0.0 reduce-scatter.2.cloned.1.call-update
  366.5 11.3 %convolution_convert_fusion.1 = bf16[768,4096]{1,0:T(8,128)(2,1)} fusion(bf16[1,4096,768]{2,1,0:T(8,128)(2,1)} %all-gather.2.cloned.1.call-done, bf16[768,768]{1,0:T(8,128)(2,1)S(1)} %bitcast.54, f32[768,768]{1,0:T(8,128)} %fusion.7), kind=kOutput, calls=%fused_computation.7 | convolution fusion | flops 4840882176 | bytes 16121856 | tf_op jit(solution)/shard_map/dot_general | solution.py:93
  377.9 5.9 all-to-all-start.2
  383.8 4.8 convert_element_type.48
  388.5 2.4 collective-permute-start.1
  390.9 4.8 convert_element_type.52
  395.7 0.6 collective-permute-start.2
  396.2 245.7 %all-to-all-done.2 = bf16[16,48,4096]{2,1,0:T(8,128)(2,1)} async-done(((bf16[16,48,4096]{2,1,0:T(8,128)(2,1)}), bf16[16,48,4096]{2,1,0:T(8,128)(2,1)}, u32[]{:S(2)}, u32[]{:S(2)}) %all-to-all-start.2) | async-done | bytes 6291488 | tf_op jit(solution)/shard_map/all_to_all | solution.py:96
  641.9 12.2 %gather_fusion.2 = bf16[512,4096]{1,0:T(8,128)(2,1)} fusion(bf16[768,4096]{1,0:T(8,128)(2,1)} %bitcast.11, s32[1024]{0:T(1024)S(1)} %pad_clamp_fusion), kind=kCustom, calls=%fused_computation.2 | custom fusion | bytes 8390656 | tf_op jit(solution)/shard_map/gather | solution.py:103
  654.0 5.8 bitcast_reduce_fusion
  659.9 64.7 %collective-permute-done.1 = bf16[1,2048,768]{2,1,0:T(8,128)(2,1)} collective-permute-done((bf16[1,2048,768]{2,1,0:T(8,128)(2,1)}, bf16[1,2048,768]{2,1,0:T(8,128)(2,1)}, u32[]{:S(2)}, u32[]{:S(2)}) %collective-permute-start.1) | collective-permute-done | bytes 3145760 | tf_op jit(solution)/shard_map/ppermute | solution.py:10
  724.6 66.3 %collective-permute-done.2 = bf16[1,2048,768]{2,1,0:T(8,128)(2,1)} collective-permute-done((bf16[1,2048,768]{2,1,0:T(8,128)(2,1)}, bf16[1,2048,768]{2,1,0:T(8,128)(2,1)}, u32[]{:S(2)}, u32[]{:S(2)}) %collective-permute-start.2) | collective-permute-done | bytes 3145760 | tf_op jit(solution)/shard_map/ppermute | solution.py:10
  791.0 0.0 reduce-scatter.2.cloned.1.call-done
  791.0 0.0 copy-start.1
  791.0 10.8 %fusion.9 = bf16[1,2048,768]{2,1,0:T(8,128)(2,1)} fusion(f32[1,2048,768]{2,1,0:T(8,128)} %param.15, bf16[1,2048,768]{2,1,0:T(8,128)(2,1)} %collective-permute-done.2, bf16[2048,768]{1,0:T(8,128)(2,1)} %reduce-scatter.2.cloned.1.call-done, f32[1,2048,768]{2,1,0:T(8,128)} %param.14, bf16[1,2048,768]{2,1,0:T(8,128)(2,1)} %collective-permute-done.1, pred[]{:T(512)S(6)} %eq.101), kind=kLoop, calls=%fused_computation.20 | loop fusion | flops 23592960 | bytes 25165824 | tf_op jit(solution)/shard_map/broadcast_in_dim | solution.py:113
  801.8 0.0 copy-done.1
  (11 shorter events, 0.1 us)
Async XLA Ops:
  7.2 314.5 %copy-start = (bf16[64,8,768]{2,1,0:T(8,128)(2,1)S(1)}, bf16[64,8,768]{2,1,0:T(8,128)(2,1)}, u32[]{:S(2)}) copy-start(bf16[64,8,768]{2,1,0:T(8,128)(2,1)} %param.10) | copy-start | bytes 2359300
  33.6 292.1 %all-to-all-start.1 = ((bf16[16,48,4096]{2,1,0:T(8,128)(2,1)}), bf16[16,48,4096]{2,1,0:T(8,128)(2,1)}, u32[]{:S(2)}, u32[]{:S(2)}) async-start(bf16[16,48,4096]{2,1,0:T(8,128)(2,1)} %broadcast_select_fusion), calls=%async_computation.1 | async-start | bytes 12582912 | tf_op jit(solution)/shard_map/all_to_all | solution.py:73
  40.9 296.7 %all-gather.2.cloned.1.call-start = ((), (), s32[]{:S(2)}) async-start(), calls=%async_computation.4 | async-start | bytes 9437184 | tf_op jit(solution)/shard_map/all_gather | solution.py:51
  40.9 276.8 %collective-permute-start = (bf16[1,2048,768]{2,1,0:T(8,128)(2,1)}, bf16[1,2048,768]{2,1,0:T(8,128)(2,1)}, u32[]{:S(2)}, u32[]{:S(2)}) collective-permute-start(bf16[1,2048,768]{2,1,0:T(8,128)(2,1)} %param.13), channel_id=1, source_target_pairs={{8,0},{9,1},{10,2},{11,3},{12,4},{13,5},{14,6},{15,7},{0,8},{1,9},... | collective-permute-start | bytes 9437192 | tf_op jit(solution)/shard_map/ppermute | solution.py:10
  325.7 30.8 %all-to-all-start = ((bf16[16,48,768]{2,1,0:T(8,128)(2,1)}), bf16[16,48,768]{2,1,0:T(8,128)(2,1)S(1)}, u32[]{:S(2)}, u32[]{:S(2)}) async-start(bf16[16,48,768]{2,1,0:T(8,128)(2,1)} %broadcast_select_fusion.2), calls=%async_computation | async-start | bytes 2359296 | tf_op jit(solution)/shard_map/all_to_all | solution.py:80
  330.4 460.5 %reduce-scatter.2.cloned.1.call-start = ((), (), s32[]{:S(2)}) async-start(), calls=%async_computation.5 | async-start | bytes 9437184 | tf_op jit(solution)/shard_map/reduce_scatter | solution.py:105
  377.9 264.0 %all-to-all-start.2 = ((bf16[16,48,4096]{2,1,0:T(8,128)(2,1)}), bf16[16,48,4096]{2,1,0:T(8,128)(2,1)}, u32[]{:S(2)}, u32[]{:S(2)}) async-start(bf16[16,48,4096]{2,1,0:T(8,128)(2,1)} %bitcast.51), calls=%async_computation.2 | async-start | bytes 12582912 | tf_op jit(solution)/shard_map/all_to_all | solution.py:96
  388.5 336.1 %collective-permute-start.1 = (bf16[1,2048,768]{2,1,0:T(8,128)(2,1)}, bf16[1,2048,768]{2,1,0:T(8,128)(2,1)}, u32[]{:S(2)}, u32[]{:S(2)}) collective-permute-start(bf16[1,2048,768]{2,1,0:T(8,128)(2,1)} %convert_element_type.48), channel_id=1, source_target_pairs={{8,0},{9,1},{10,2},{11,3},{12,4},{13,5},{14,6},{15,7},{0,8},{1,9},... | collective-permute-start | bytes 9437192 | tf_op jit(solution)/shard_map/ppermute | solution.py:10
  395.7 395.3 %collective-permute-start.2 = (bf16[1,2048,768]{2,1,0:T(8,128)(2,1)}, bf16[1,2048,768]{2,1,0:T(8,128)(2,1)}, u32[]{:S(2)}, u32[]{:S(2)}) collective-permute-start(bf16[1,2048,768]{2,1,0:T(8,128)(2,1)} %convert_element_type.52), channel_id=1, source_target_pairs={{8,0},{9,1},{10,2},{11,3},{12,4},{13,5},{14,6},{15,7},{0,8},{1,9},... | collective-permute-start | bytes 9437192 | tf_op jit(solution)/shard_map/ppermute | solution.py:10
  791.0 10.8 %copy-start.1 = (bf16[64,8,768]{2,1,0:T(8,128)(2,1)S(1)}, bf16[64,8,768]{2,1,0:T(8,128)(2,1)}, u32[]{:S(2)}) copy-start(bf16[64,8,768]{2,1,0:T(8,128)(2,1)} %param.10) | copy-start | bytes 2359300
Sparse Core Ops, SparseCore 0:
  321.8 15.7 all-gather.1
  366.7 14.5 reduce-scatter.1
where the time goes:
time: 810 us; the launch traced here: 809 us
  waiting for transfers between devices  666 us (82%)
  other arithmetic  41 us (5%)
  local copies, waits for them, and re-layouts  31.6 us (4%)
  matrix products  31.3 us (4%)
  starting transfers between devices  23.6 us (3%)
  between operations  14.8 us (2%)
    ppermute x3, waiting for transfers between devices, passed_along(): return lax.ppermute(block, axis, route)  405 us
    all_to_all x1, waiting for transfers between devices, body(): lax.all_to_all(back_rows.reshape(count_dev, capacity, width), 'expert', s...  246 us
  transfers between devices with their start and end apart: 8, of which 6 were waited for; matrix products, arithmetic and copies ran while one was open for 7% of the time, Pallas kernels for 0%

commit v1 on v0

v1 whole, which is shorter than its diff:
```python
import itertools

import jax
import jax.numpy as jnp
from jax import lax
from jax.sharding import PartitionSpec as P


def adam_direction(grad, first, second):
    first_new = 0.9 * first + 0.1 * grad
    second_new = 0.95 * second + 0.05 * grad * grad
    return (first_new / (jnp.sqrt(second_new) + 1e-08)).astype(jnp.bfloat16)


def swap_slots(block, swap_mask, here):
    count = swap_mask.shape[0]
    half = count // 2
    pairs = max(1, count // 8)
    lower = swap_mask[:half]
    moving = jnp.sum(jnp.where(jnp.arange(count) == here, swap_mask, 0)) == 1
    choices = list(itertools.combinations(range(half), pairs)) if half <= 8 else None
    if choices is None:
        got = lax.ppermute(block, "expert", [(i, (i + half) % count) for i in range(count)])
        return jnp.where(moving, got, block)

    def branch(chosen):
        route = [(p, p + half) for p in chosen] + [(p + half, p) for p in chosen]

        def run(value):
            return jnp.where(moving, lax.ppermute(value, "expert", route), value)

        return run

    table = jnp.array([[int(p in c) for p in range(half)] for c in choices], jnp.int32)
    fits = jnp.all(table == lower[None, :], axis=1).astype(jnp.int32)
    number = jnp.sum(fits * jnp.arange(len(choices), dtype=jnp.int32))
    return lax.switch(number, [branch(c) for c in choices], block)


def body(
    tokens, token_experts, hidden_grad, held_expert, swap_mask, weight, first_moment, second_moment
):
    count_dev = lax.axis_size("expert")
    n_dp = lax.axis_size("dp")
    here = lax.axis_index("expert")
    row = lax.axis_index("dp")
    tok_dev, top = token_experts.shape
    hidden = hidden_grad.shape[2]
    rows_x = lax.all_gather(tokens, "expert", axis=0, tiled=True)
    full_w = lax.all_gather(weight[0], "dp", axis=0, tiled=True)
    named = token_experts[None, :, :] == held_expert[:, None, None]
    same = jnp.eye(tok_dev, dtype=jnp.bool_)
    place = (same[None, :, :, None] & named[:, None, :, :]).astype(jnp.bfloat16)
    send_g = jnp.dot(
        place.reshape(count_dev * tok_dev, tok_dev * top),
        hidden_grad.reshape(tok_dev * top, hidden),
        preferred_element_type=jnp.float32,
    ).astype(jnp.bfloat16)
    rows_g = lax.all_to_all(
        send_g.reshape(count_dev, tok_dev, hidden), "expert", split_axis=0, concat_axis=0, tiled=True
    ).reshape(count_dev * tok_dev, hidden)
    pre = jnp.dot(rows_x, full_w, preferred_element_type=jnp.float32)
    sig = jax.nn.sigmoid(pre)
    grad_pre = (rows_g.astype(jnp.float32) * sig * (1.0 + pre * (1.0 - sig))).astype(jnp.bfloat16)
    partial = lax.dot_general(
        rows_x, grad_pre, (((0,), (0,)), ((), ())), preferred_element_type=jnp.float32
    ).astype(jnp.bfloat16)
    if n_dp == 2:
        depth = partial.shape[0] // 2
        mine = lax.dynamic_slice_in_dim(partial, row * depth, depth, 0)
        other = lax.dynamic_slice_in_dim(partial, (1 - row) * depth, depth, 0)
        got = lax.ppermute(other, "dp", [(0, 1), (1, 0)])
        expert_grad = mine.astype(jnp.float32) + got.astype(jnp.float32)
    else:
        expert_grad = lax.psum_scatter(
            partial, "dp", scatter_dimension=0, tiled=True
        ).astype(jnp.float32)
    back_rows = lax.dot_general(
        grad_pre, full_w, (((1,), (1,)), ((), ())), preferred_element_type=jnp.float32
    ).astype(jnp.bfloat16)
    token_grad = lax.psum_scatter(back_rows, "expert", scatter_dimension=0, tiled=True)
    adam_step = adam_direction(expert_grad, first_moment[0], second_moment[0])
    adam_step = swap_slots(adam_step, swap_mask, here)[None]
    return (token_grad, adam_step)


def solution(mesh):
    in_specs = (
        P(("dp", "expert"), None),
        P(("dp", "expert"), None),
        P(("dp", "expert"), None, None),
        P(),
        P(),
        P("expert", "dp", None),
        P("expert", "dp", None),
        P("expert", "dp", None),
    )
    out_specs = (P(("dp", "expert"), None), P("expert", "dp", None))
    return jax.shard_map(body, mesh=mesh, in_specs=in_specs, out_specs=out_specs, check_vma=False)
```

time: 810 us -> 370 us (0.46)
  waiting for transfers between devices: 666 us -> 258 us
  other arithmetic: 41 us -> 15.7 us
  starting transfers between devices: 23.6 us -> 9.88 us
    ppermute x3 -> x2, waiting for transfers between devices: 405 us -> 0.01 us  [the longest x1 0.01 us: body(): got = lax.ppermute(other, 'dp', [(0, 1), (1, 0)])]
    all_to_all x3 -> x1, waiting for transfers between devices: 255 us -> 0.01 us  [body(): lax.all_to_all(send_g.reshape(count_dev, tok_dev, hidden), 'expert', spli...]
    all_gather x1 -> x2, waiting for transfers between devices: 6.88 us -> 132 us  [the longest x1 127 us: body(): rows_x = lax.all_gather(tokens, 'expert', axis=0, tiled=True)]
    reduce_scatter x1, waiting for transfers between devices: 0.01 us -> 124 us  [body(): lax.psum_scatter(back_rows, 'expert', scatter_dimension=0, tiled=True)]
    gather x3 -> x0, local copies, waits for them, and re-layouts: 28 us -> none  [the longest x1 13 us: body(): tokens[source_row // top]]
    unnamed x5 -> x17, local copies, waits for them, and re-layouts: 0.79 us -> 15.8 us
    select_n x7 -> x0, other arithmetic: 12.4 us -> none  [the longest x1 5.93 us: body(): jnp.where(filled[:, None], tokens[source_row // top], jnp.zeros((), token...]
    all_to_all x3 -> x1, starting transfers between devices: 18 us -> 7.28 us  [body(): lax.all_to_all(send_g.reshape(count_dev, tok_dev, hidden), 'expert', spli...]
  transfers between devices with their start and end apart: 8 -> 6, of which waited for: 6 -> 3; matrix products, arithmetic and copies ran while one was open for 7% -> 18% of each run, Pallas kernels for 0% -> 0%
where the time goes in v1:
time: 370 us; the launch traced here: 363 us
  waiting for transfers between devices  258 us (70%)
  matrix products  39.3 us (11%)
  local copies, waits for them, and re-layouts  25 us (7%)
  other arithmetic  15.7 us (4%)
  between operations  15.2 us (4%)
  starting transfers between devices  9.88 us (3%)
    all_gather x1, waiting for transfers between devices, body(): rows_x = lax.all_gather(tokens, 'expert', axis=0, tiled=True)  127 us
    reduce_scatter x1, waiting for transfers between devices, body(): lax.psum_scatter(back_rows, 'expert', scatter_dimension=0, tiled=True)  124 us
    unnamed x17, local copies, waits for them, and re-layouts  15.8 us
    dot_general x1, matrix products, body(): lax.dot_general(grad_pre, full_w, (((1,), (1,)), ((), ())), preferred_ele...  13.7 us
    dot_general x1, matrix products, body(): pre = jnp.dot(rows_x, full_w, preferred_element_type=jnp.float32)  12 us
    dot_general x1, matrix products, body(): lax.dot_general(rows_x, grad_pre, (((0,), (0,)), ((), ())), preferred_ele...  11.4 us
    convert_element_type x1, other arithmetic, adam_direction(): return (first_new / (jnp.sqrt(second_new) + 1e-08)).astype(jnp.bfloat16)  8.86 us
  transfers between devices with their start and end apart: 6, of which 3 were waited for; matrix products, arithmetic and copies ran while one was open for 18% of the time, Pallas kernels for 0%

profile of v1, /device:TPU:4, one launch (start us, length us, event | category | flops | bytes accessed | tf_op | source)
XLA Modules:
  0.0 363.0 jit_solution(5950345792816573546)
XLA Ops:
  7.2 0.0 copy-start
  7.2 0.0 copy-start.3
  7.2 0.0 copy-start.5
  7.2 0.0 all-gather.6.cloned.1.call-start
  7.2 0.7 all-gather.6.cloned.1.call-update
  7.9 0.0 all-gather.4.cloned.1.call-start
  8.0 0.7 all-gather.4.cloned.1.call-update
  8.7 0.0 copy-done.3
  8.7 0.1 copy.73
  8.8 0.0 copy-done.5
  8.8 0.1 broadcast_compare_fusion
  8.9 1.4 broadcast_and_fusion
  10.4 2.4 and.28
  12.7 0.0 copy-done
  12.7 2.2 convolution_convert_fusion.2
  15.0 7.3 %all-to-all-start = ((bf16[16,64,768]{2,1,0:T(8,128)(2,1)}), bf16[16,64,768]{2,1,0:T(8,128)(2,1)S(1)}, u32[]{:S(2)}, u32[]{:S(2)}) async-start(bf16[16,64,768]{2,1,0:T(8,128)(2,1)} %bitcast.1), calls=%async_computation | async-start | bytes 3145728 | tf_op jit(solution)/shard_map/all_to_all | solution.py:59
  22.2 0.2 reduce-scatter.2.cloned.1.call-start
  22.5 5.4 %all-gather.6.cloned.1.call-done = bf16[1,4096,768]{2,1,0:T(8,128)(2,1)} async-done(((bf16[1,2048,768]{2,1,0:T(8,128)(2,1)}), bf16[1,4096,768]{2,1,0:T(8,128)(2,1)}) %all-gather.6.cloned.1.call-update) | async-done | bytes 6291472 | tf_op jit(solution)/shard_map/all_gather | solution.py:50
  27.8 127.0 %all-gather.4.cloned.1.call-done = bf16[1024,4096]{1,0:T(8,128)(2,1)} async-done(((bf16[64,4096]{1,0:T(8,128)(2,1)}), bf16[1024,4096]{1,0:T(8,128)(2,1)}) %all-gather.4.cloned.1.call-update) | async-done | bytes 8388624 | tf_op jit(solution)/shard_map/all_gather | solution.py:49
  154.8 12.0 %fusion.5 = f32[1024,768]{1,0:T(8,128)} fusion(bf16[1024,4096]{1,0:T(8,128)(2,1)} %all-gather.4.cloned.1.call-done, bf16[1,4096,768]{2,1,0:T(8,128)(2,1)} %all-gather.6.cloned.1.call-done), kind=kOutput, calls=%fused_computation.10 | convolution fusion | flops 6442450944 | bytes 17825792 | tf_op jit(solution)/shard_map/dot_general | solution.py:62
  166.9 0.0 all-to-all-done
  166.9 13.7 %convolution_convert_fusion = bf16[1024,4096]{1,0:T(8,128)(2,1)} fusion(bf16[1,4096,768]{2,1,0:T(8,128)(2,1)} %all-gather.6.cloned.1.call-done, bf16[1024,768]{1,0:T(8,128)(2,1)S(1)} %bitcast.39, f32[1024,768]{1,0:T(8,128)} %fusion.5), kind=kOutput, calls=%fused_computation.1 | convolution fusion | flops 6454509568 | bytes 19398656 | tf_op jit(solution)/shard_map/dot_general | solution.py:78
  180.5 0.0 reduce-scatter.2.cloned.1.call-update
  180.6 11.4 %convolution_convert_fusion.1 = bf16[768,4096]{1,0:T(8,128)(2,1)S(1)} fusion(bf16[1024,4096]{1,0:T(8,128)(2,1)} %all-gather.4.cloned.1.call-done, bf16[1024,768]{1,0:T(8,128)(2,1)S(1)} %bitcast.40, f32[1024,768]{1,0:T(8,128)} %fusion.5), kind=kOutput, calls=%fused_computation.2 | convolution fusion | flops 6453460992 | bytes 19398656 | tf_op jit(solution)/shard_map/dot_general | solution.py:65
  192.0 0.0 copy-start.2
  192.0 0.0 copy-start.6
  192.0 0.2 dynamic-slice_bitcast_fusion
  192.2 2.4 copy-done.2
  194.7 0.0 collective-permute-start.28
  194.7 0.0 copy-done.6
  194.7 0.6 fusion.15
  196.0 6.6 %copy.74 = f32[1,2048,768]{1,2,0:T(8,128)} copy(f32[1,2048,768]{2,1,0:T(8,128)} %param.43) | data formatting | bytes 12582912 | tf_op args[6]
  202.6 0.0 copy-start.4
  202.6 6.6 %copy.75 = f32[1,2048,768]{1,2,0:T(8,128)} copy(f32[1,2048,768]{2,1,0:T(8,128)} %param.44) | data formatting | bytes 12582912 | tf_op args[7]
  209.2 0.0 copy-done.4
  209.2 0.1 compare_reduce_fusion
  209.3 0.6 select_reduce_fusion
  210.6 0.0 collective-permute-done.28
  210.6 8.9 %fusion.7 = bf16[2048,768]{0,1:T(8,128)(2,1)S(1)} fusion(f32[1,2048,768]{1,2,0:T(8,128)} %copy.75, bf16[2048,768]{0,1:T(8,128)(2,1)} %collective-permute-done.28, f32[1,2048,768]{1,2,0:T(8,128)} %copy.74, bf16[768,4096]{1,0:T(8,128)(2,1)} %copy-done.2, s32[]{:T(128)S(6)} %select_n.74), kind=kLoop, calls=%fused_computation.12 | loop fusion | flops 20447232 | bytes 22020100 | tf_op jit(solution)/shard_map/convert_element_type | solution.py:12
  219.5 9.3 %conditional.1 = (bf16[2048,768]{1,0:T(8,128)(2,1)}, bf16[2048,768]{1,0:T(8,128)(2,1)}, bf16[2048,768]{1,0:T(8,128)(2,1)}, pred[]{:T(512)}) conditional(s32[]{:T(128)} %clamp.3, (bf16[2048,768]{0,1:T(8,128)(2,1)S(1)}, pred[]{:T(512)}) %tuple.149, (bf16[2048,768]{0,1:T(8,128)(2,1)S(1)}, pred[]{:T(512)}) %tuple.149, ...), branch_computations={%region_4.5_spmd, %region_5.6_spmd, %region_6.7_spmd, %region_7.8_... | conditional | bytes 25165896 | solution.py:37
  219.8 2.8 copy.96
  222.6 2.3 collective-permute-start.20
  224.9 3.8 %copy.166 = bf16[2048,768]{1,0:T(8,128)(2,1)} copy(bf16[2048,768]{1,0:T(8,128)(2,1)} %copy.96) | data formatting | bytes 6291456 | tf_op jit(solution)/shard_map/cond
  228.8 0.0 collective-permute-done.20
  228.8 0.0 copy-start.1
  228.8 4.0 %select_bitcast_fusion = bf16[1,2048,768]{2,1,0:T(8,128)(2,1)} fusion(bf16[2048,768]{1,0:T(8,128)(2,1)} %get-tuple-element.179, bf16[2048,768]{1,0:T(8,128)(2,1)} %get-tuple-element.180, pred[]{:T(512)} %get-tuple-element.178), kind=kLoop, calls=%fused_computation.16 | loop fusion | flops 1572864 | bytes 9437185 | tf_op jit(solution)/shard_map/broadcast_in_dim | solution.py:83
  232.7 123.8 %reduce-scatter.2.cloned.1.call-done = bf16[64,4096]{1,0:T(8,128)(2,1)} async-done(((bf16[1024,4096]{1,0:T(8,128)(2,1)}), bf16[64,4096]{1,0:T(8,128)(2,1)}) %reduce-scatter.2.cloned.1.call-update) | async-done | bytes 524304 | tf_op jit(solution)/shard_map/reduce_scatter | solution.py:81
  356.5 0.0 copy-done.1
  (1 shorter events, 0.0 us)
Async XLA Ops:
  7.2 5.6 %copy-start = (bf16[64,8,768]{2,1,0:T(8,128)(2,1)S(1)}, bf16[64,8,768]{2,1,0:T(8,128)(2,1)}, u32[]{:S(2)}) copy-start(bf16[64,8,768]{2,1,0:T(8,128)(2,1)} %param.39) | copy-start | bytes 2359300
  7.2 1.5 copy-start.3
  7.2 1.6 copy-start.5
  7.2 20.6 %all-gather.6.cloned.1.call-start = ((), (), s32[]{:S(2)}) async-start(), calls=%async_computation.4 | async-start | bytes 9437184 | tf_op jit(solution)/shard_map/all_gather | solution.py:50
  7.9 146.9 %all-gather.4.cloned.1.call-start = ((), (), s32[]{:S(2)}) async-start(), calls=%async_computation.2 | async-start | bytes 8912896 | tf_op jit(solution)/shard_map/all_gather | solution.py:49
  15.0 151.9 %all-to-all-start = ((bf16[16,64,768]{2,1,0:T(8,128)(2,1)}), bf16[16,64,768]{2,1,0:T(8,128)(2,1)S(1)}, u32[]{:S(2)}, u32[]{:S(2)}) async-start(bf16[16,64,768]{2,1,0:T(8,128)(2,1)} %bitcast.1), calls=%async_computation | async-start | bytes 3145728 | tf_op jit(solution)/shard_map/all_to_all | solution.py:59
  22.2 334.2 %reduce-scatter.2.cloned.1.call-start = ((), (), s32[]{:S(2)}) async-start(), calls=%async_computation.3 | async-start | bytes 8912896 | tf_op jit(solution)/shard_map/reduce_scatter | solution.py:81
  192.0 2.7 copy-start.2
  192.0 2.7 copy-start.6
  194.7 15.9 %collective-permute-start.28 = (bf16[2048,768]{0,1:T(8,128)(2,1)S(1)}, bf16[2048,768]{0,1:T(8,128)(2,1)}, u32[]{:S(2)}, u32[]{:S(2)}) collective-permute-start(bf16[2048,768]{0,1:T(8,128)(2,1)S(1)} %dynamic-slice_bitcast_fusion), channel_id=1, source_target_pairs={{0,16},{16,0},{1,17},{17,1},{2,18},{18,2},{3,19},{19,3},{4,20},{20... | collective-permute-start | bytes 9437192 | tf_op jit(solution)/shard_map/ppermute | solution.py:72
  202.6 6.6 %copy-start.4 = (s32[28,8]{0,1:T(8,128)S(1)}, s32[28,8]{0,1:T(8,128)}, u32[]{:S(2)}) copy-start(s32[28,8]{0,1:T(8,128)} %constant.36.clone) | copy-start | bytes 2692
  222.6 6.1 %collective-permute-start.20 = (bf16[2048,768]{1,0:T(8,128)(2,1)}, bf16[2048,768]{1,0:T(8,128)(2,1)}, u32[]{:S(2)}, u32[]{:S(2)}) collective-permute-start(bf16[2048,768]{1,0:T(8,128)(2,1)} %copy.96), channel_id=1, source_target_pairs={{3,11},{6,14},{11,3},{14,6},{19,27},{22,30},{27,19},{30,22}} | collective-permute-start | bytes 9437192 | tf_op jit(solution)/shard_map/cond/branch_20_fun/ppermute | solution.py:30
  228.8 127.7 %copy-start.1 = (bf16[64,8,768]{2,1,0:T(8,128)(2,1)S(1)}, bf16[64,8,768]{2,1,0:T(8,128)(2,1)}, u32[]{:S(2)}) copy-start(bf16[64,8,768]{2,1,0:T(8,128)(2,1)} %param.39) | copy-start | bytes 2359300
Sparse Core Ops, SparseCore 0:
  9.6 18.2 all-gather.5
  30.6 124.1 all-gather.3
  180.7 175.7 reduce-scatter.1
